TPU v7x, 512 devices: a whole 4x4x16 slice. The times are simulated.
512 devices in a mesh: row: 16 (over x_lo, y, core), col: 32 (over x_hi, z).
Axes of the slice: x: 4 (x_hi: 2, x_lo: 2; x = x_hi * 2 + x_lo), y: 4, z: 16, core: 2. Of those that a mesh axis runs over, the one named last changes fastest.
Arguments:
- seq_ids: int32 [1024], replicated, may hold values from 0 to 3, never falling along the last dimension, each value on 1 to 512 neighbouring positions
- query_inputs: bfloat16 [1024, 8192], P('col', 'row'), may hold values from -6 to 6
- query_grads: bfloat16 [1024, 8192], P('row', 'col'), may hold values from -0.25 to 0.25
- query_act_basis: bfloat16 [8192, 8192], P('row', 'col'), may hold values from -0.0625 to 0.0625
- query_grad_basis: bfloat16 [8192, 8192], P('col', 'row'), may hold values from -0.0625 to 0.0625
- output_inputs: bfloat16 [1024, 8192], P('col', 'row'), may hold values from -6 to 6
- output_grads: bfloat16 [1024, 8192], P('row', 'col'), may hold values from -0.25 to 0.25
- output_act_basis: bfloat16 [8192, 8192], P('row', 'col'), may hold values from -0.0625 to 0.0625
- output_grad_basis: bfloat16 [8192, 8192], P('col', 'row'), may hold values from -0.0625 to 0.0625
Outputs:
- query_corr: float32 [8192, 8192], P('row', 'col')
- output_corr: float32 [8192, 8192], P('row', 'col')
Inputs may be any that keep to these rules, and one draw needn't show every extreme that they name: seq_ids never falls along the tokens; each of the 4 sequences holds 1 to 512 tokens, and one holds exactly 512.
All inputs are finite; a program needn't handle non-finite values.
Results may differ from a plain program's by a relative error of at most 0.0003.
Values may be sent and summed in bfloat16 or wider, within the bound.
No kernel may reach another device: no remote copies, remote signals or barrier semaphores. Data moves between devices by JAX's collectives and lax.ppermute only.
A program may use at most 64 MiB of HBM per device.

v0:
```python
import jax
import jax.numpy as jnp
from jax import lax
from jax.sharding import Mesh, PartitionSpec as P

SEQS = 4
ROW = ("xl", "y", "c")
Z = ("zh", "zl")
PLANE = ("xh", "xl", "y", "c")
NZ = 16
NEAR = (0, 1, -1, 2)
FAR = (0, 4, -4, 8)
TOP = 32000.0


def shift(x, by):
    if by == 0:
        return x
    return lax.ppermute(x, Z, [(i, (i + by) % NZ) for i in range(NZ)])


def swap_half(x):
    return lax.ppermute(x, "xh", [(0, 1), (1, 0)])


def pack(x):
    b, p, t, n = x.shape
    most = jnp.max(jnp.abs(x), axis=(2, 3), keepdims=True)
    step = jnp.ceil(jnp.log2(jnp.maximum(most, 1e-30)) * 64.0)
    codes = jnp.round(x * (TOP * jnp.exp2(step * (-1.0 / 64.0)))).astype(jnp.int16)
    head = jnp.broadcast_to(step.astype(jnp.int16), (b, p, 4, n))
    return jnp.concatenate([codes.reshape(b, p * t, n), head.reshape(b, 8, n)], axis=1)


def unpack(w):
    b, rows, n = w.shape
    t = (rows - 8) // 2
    step = jnp.stack([w[:, rows - 8, :1], w[:, rows - 4, :1]], axis=1).astype(jnp.float32)
    scale = jnp.exp2(step * (1.0 / 64.0)) * (1.0 / TOP)
    return w[:, : 2 * t].reshape(b, 2, t, n).astype(jnp.float32) * scale[..., None]


def roll_blocks(x, by):
    return lax.dynamic_slice_in_dim(jnp.concatenate([x, x], 0), by, x.shape[0], 0)


def reduce_scatter_z(part):

    def group(near):
        return jnp.stack([part[(near + far) % NZ] for far in FAR])

    total = group(0)
    for near in NEAR[1:]:
        total = total + unpack(shift(pack(group(near)), near))
    result = total[0]
    for index, far in enumerate(FAR[1:]):
        result = result + unpack(shift(pack(total[index + 1 : index + 2]), far))[0]
    return result


def gather_z(w):
    level = jnp.concatenate([shift(w, far) for far in FAR], 0)
    both = jnp.concatenate([shift(level, near) for near in NEAR], 0)
    offsets = [(near + far) % NZ for near in NEAR for far in FAR]
    order = [offsets.index(i) for i in range(NZ)]
    return jnp.concatenate([both[k : k + 1] for k in order], 0)


def correct(act_rot, grad_rot, seq_ids):
    running = jnp.zeros((grad_rot.shape[1], act_rot.shape[1]), jnp.float32)
    for seq in range(SEQS):
        grad_rows = jnp.where((seq_ids == seq)[:, None], grad_rot, 0.0)
        product = lax.dot_general(
            grad_rows, act_rot, (((0,), (0,)), ((), ())), precision=lax.Precision.HIGH
        )
        running = running + product * product
    return running / SEQS


def dot(a, b):
    return jnp.dot(a, b, preferred_element_type=jnp.float32)


def per_device(seq_ids, qx, qg, qa, qb, ox, og, oa, ob):
    z = lax.axis_index(Z)
    xh = lax.axis_index("xh")
    mine_first = xh == 0
    grads = jnp.stack([qg, og])
    sent = jnp.transpose(grads.reshape(2, 2, 32, 256), (1, 0, 2, 3))
    sent = jnp.broadcast_to(sent[:, None], (2, 16, 2, 32, 256)).reshape(32, 2, 32, 256)
    got = lax.all_to_all(sent, PLANE, split_axis=0, concat_axis=0, tiled=True)
    grad_basis = jnp.stack([qb, ob])
    grad_other = swap_half(grad_basis)
    inputs = lax.all_gather(jnp.stack([qx, ox])[None], Z, axis=0, tiled=True)
    act_basis = jnp.stack([qa, oa])
    act_other = swap_half(act_basis)
    got = got.reshape(2, 16, 2, 32, 256)
    g0 = roll_blocks(got[0], z)
    g1 = roll_blocks(got[1], z)
    b0 = jnp.where(mine_first, grad_basis, grad_other)
    b1 = jnp.where(mine_first, grad_other, grad_basis)
    parts = []
    for p in range(2):
        part = dot(g0[:, p].reshape(512, 256), b0[p]) + dot(g1[:, p].reshape(512, 256), b1[p])
        parts.append(part.reshape(16, 32, 512))
    part = jnp.stack(parts, 1)
    grad_mine = reduce_scatter_z(part)
    words = gather_z(pack(grad_mine[None]))
    others = swap_half(words)
    a0 = jnp.where(mine_first, act_basis, act_other)
    a1 = jnp.where(mine_first, act_other, act_basis)
    parts = []
    for p in range(2):
        rows = inputs[:, p].reshape(512, 512)
        part = jnp.concatenate([dot(rows, a0[p]), dot(rows, a1[p])], 1)
        parts.append(part.reshape(16, 32, 512))
    act_words = pack(jnp.stack(parts, 1))
    act_words = lax.all_to_all(act_words, ROW, split_axis=0, concat_axis=0, tiled=True)
    act_mine = jnp.sum(unpack(act_words), axis=0)
    act_sent = pack(jnp.stack([act_mine[:, :, :256], act_mine[:, :, 256:]]))
    act_sent = jnp.broadcast_to(act_sent[:, None], (2, 16, 72, 256)).reshape(32, 72, 256)
    act_words = lax.all_to_all(act_sent, PLANE, split_axis=0, concat_axis=0, tiled=True)
    act = jnp.transpose(unpack(act_words), (1, 0, 2, 3)).reshape(2, 1024, 256)
    low = jnp.where(mine_first, words, others)
    high = jnp.where(mine_first, others, words)
    both = jnp.stack([low, high])
    both = lax.rev(both, (1,))
    both = lax.dynamic_slice_in_dim(jnp.concatenate([both, both], 1), NZ - 1 - z, NZ, 1)
    grad = unpack(both.reshape(32, 72, 512)).reshape(2, 16, 2, 32, 512)
    grad = jnp.transpose(grad, (2, 1, 0, 3, 4)).reshape(2, 1024, 512)
    return (correct(act[0], grad[0], seq_ids), correct(act[1], grad[1], seq_ids))


def solution(mesh):
    fine = Mesh(mesh.devices.reshape(2, 4, 2, 2, 4, 4), ("xl", "y", "c", "xh", "zh", "zl"))
    row, col = (ROW, ("xh",) + Z)
    in_specs = (P(), P(col, row), P(row, col), P(row, col), P(col, row)) + (
        P(col, row),
        P(row, col),
        P(row, col),
        P(col, row),
    )
    out_specs = (P(row, col), P(row, col))
    return jax.shard_map(
        per_device, mesh=fine, in_specs=in_specs, out_specs=out_specs, check_vma=False
    )
```

profile of v0, /device:TPU:1, one launch (start us, length us, event | category | flops | bytes accessed | tf_op | source)
XLA Modules:
  0.0 297.2 jit_solution(14725430089309707744)
XLA Ops:
  9.2 10.5 %all-to-all-start = ((bf16[32,2,32,256]{3,2,1,0:T(8,128)(2,1)}), bf16[32,2,32,256]{3,2,1,0:T(8,128)(2,1)S(1)}, u32[]{:S(2)}, u32[]{:S(2)}) async-start(bf16[32,2,32,256]{3,2,1,0:T(8,128)(2,1)} %bitcast.3), calls=%async_computation | async-start | bytes 2097152 | tf_op jit(solution)/shard_map/all_to_all | solution.py:91
  19.8 4.9 %collective-permute-start = (bf16[2,256,512]{2,1,0:T(8,128)(2,1)S(1)}, bf16[2,256,512]{2,1,0:T(8,128)(2,1)}, u32[]{:S(2)}, u32[]{:S(2)}) collective-permute-start(bf16[2,256,512]{2,1,0:T(8,128)(2,1)S(1)} %pad_maximum_fusion.3), channel_id=1, source_target_pairs={{0,16},{16,0},{1,17},{17,1},{2,18},{18,2},{3,19},{19,3},{4,20},{20... | collective-permute-start | bytes 1572872 | tf_op jit(solution)/shard_map/ppermute | solution.py:23
  25.5 1.9 collective-permute-start.14
  27.5 18.6 %collective-permute-done = bf16[2,256,512]{2,1,0:T(8,128)(2,1)} collective-permute-done((bf16[2,256,512]{2,1,0:T(8,128)(2,1)S(1)}, bf16[2,256,512]{2,1,0:T(8,128)(2,1)}, u32[]{:S(2)}, u32[]{:S(2)}) %collective-permute-start) | collective-permute-done | bytes 524320 | tf_op jit(solution)/shard_map/ppermute | solution.py:23
  49.9 2.9 collective-permute-start.3
  53.6 8.2 %collective-permute-start.2 = (s16[4,72,512]{2,1,0:T(8,128)(2,1)S(1)}, s16[4,72,512]{2,1,0:T(8,128)(2,1)S(1)}, u32[]{:S(2)}, u32[]{:S(2)}) collective-permute-start(s16[4,72,512]{2,1,0:T(8,128)(2,1)S(1)} %pad_add_fusion.3), channel_id=1, source_target_pairs={{0,15},{1,0},{2,1},{3,2},{4,3},{5,4},{6,5},{7,6},{8,7},{9,8},{10,9... | collective-permute-start | bytes 884744 | tf_op jit(solution)/shard_map/ppermute | solution.py:19
  62.5 1.9 collective-permute-start.1
  64.4 2.7 collective-permute-done.3
  67.8 11.0 %collective-permute-done.1 = s16[4,72,512]{2,1,0:T(8,128)(2,1)} collective-permute-done((s16[4,72,512]{2,1,0:T(8,128)(2,1)S(1)}, s16[4,72,512]{2,1,0:T(8,128)(2,1)}, u32[]{:S(2)}, u32[]{:S(2)}) %collective-permute-start.1) | collective-permute-done | bytes 294944 | tf_op jit(solution)/shard_map/ppermute | solution.py:19
  81.9 9.4 %collective-permute-start.6 = (s16[1,72,512]{2,1,0:T(8,128)(2,1)S(1)}, s16[1,72,512]{2,1,0:T(8,128)(2,1)S(1)}, u32[]{:S(2)}, u32[]{:S(2)}) collective-permute-start(s16[1,72,512]{2,1,0:T(8,128)(2,1)S(1)} %pad_add_fusion.8), channel_id=1, source_target_pairs={{0,8},{1,9},{2,10},{3,11},{4,12},{5,13},{6,14},{7,15},{8,0},{9,1},... | collective-permute-start | bytes 221192 | tf_op jit(solution)/shard_map/ppermute | solution.py:19
  91.6 1.9 collective-permute-start.5
  93.9 7.3 %collective-permute-start.4 = (s16[1,72,512]{2,1,0:T(8,128)(2,1)S(1)}, s16[1,72,512]{2,1,0:T(8,128)(2,1)S(1)}, u32[]{:S(2)}, u32[]{:S(2)}) collective-permute-start(s16[1,72,512]{2,1,0:T(8,128)(2,1)S(1)} %pad_add_fusion.6), channel_id=1, source_target_pairs={{0,4},{1,5},{2,6},{3,7},{4,8},{5,9},{6,10},{7,11},{8,12},{9,13},{1... | collective-permute-start | bytes 221192 | tf_op jit(solution)/shard_map/ppermute | solution.py:19
  103.1 2.1 collective-permute-done.5
  111.1 9.1 %collective-permute-start.9 = (s16[1,72,512]{2,1,0:T(8,128)(2,1)S(1)}, s16[1,72,512]{2,1,0:T(8,128)(2,1)S(1)}, u32[]{:S(2)}, u32[]{:S(2)}) collective-permute-start(s16[1,72,512]{2,1,0:T(8,128)(2,1)S(1)} %get-tuple-element.74), channel_id=1, source_target_pairs={{0,8},{1,9},{2,10},{3,11},{4,12},{5,13},{6,14},{7,15},{8,0},{9,1},... | collective-permute-start | bytes 221192 | tf_op jit(solution)/shard_map/ppermute | solution.py:19
  120.2 4.1 %collective-permute-start.8 = (s16[1,72,512]{2,1,0:T(8,128)(2,1)S(1)}, s16[1,72,512]{2,1,0:T(8,128)(2,1)S(1)}, u32[]{:S(2)}, u32[]{:S(2)}) collective-permute-start(s16[1,72,512]{2,1,0:T(8,128)(2,1)S(1)} %get-tuple-element.74), channel_id=1, source_target_pairs={{0,12},{1,13},{2,14},{3,15},{4,0},{5,1},{6,2},{7,3},{8,4},{9,5},{1... | collective-permute-start | bytes 221192 | tf_op jit(solution)/shard_map/ppermute | solution.py:19
  124.3 5.1 %collective-permute-start.7 = (s16[1,72,512]{2,1,0:T(8,128)(2,1)S(1)}, s16[1,72,512]{2,1,0:T(8,128)(2,1)S(1)}, u32[]{:S(2)}, u32[]{:S(2)}) collective-permute-start(s16[1,72,512]{2,1,0:T(8,128)(2,1)S(1)} %get-tuple-element.74), channel_id=1, source_target_pairs={{0,4},{1,5},{2,6},{3,7},{4,8},{5,9},{6,10},{7,11},{8,12},{9,13},{1... | collective-permute-start | bytes 221192 | tf_op jit(solution)/shard_map/ppermute | solution.py:19
  129.4 4.0 %collective-permute-done.8 = s16[1,72,512]{2,1,0:T(8,128)(2,1)S(1)} collective-permute-done((s16[1,72,512]{2,1,0:T(8,128)(2,1)S(1)}, s16[1,72,512]{2,1,0:T(8,128)(2,1)S(1)}, u32[]{:S(2)}, u32[]{:S(2)}) %collective-permute-start.8) | collective-permute-done | bytes 73760 | tf_op jit(solution)/shard_map/ppermute | solution.py:19
  134.1 1.9 collective-permute-start.10
  136.7 1.9 collective-permute-start.11
  139.7 4.6 %collective-permute-start.12 = (s16[4,72,512]{2,1,0:T(8,128)(2,1)S(1)}, s16[4,72,512]{2,1,0:T(8,128)(2,1)S(1)}, u32[]{:S(2)}, u32[]{:S(2)}) collective-permute-start(s16[4,72,512]{2,1,0:T(8,128)(2,1)S(1)} %pad_add_fusion.5), channel_id=1, source_target_pairs={{0,15},{1,0},{2,1},{3,2},{4,3},{5,4},{6,5},{7,6},{8,7},{9,8},{10,9... | collective-permute-start | bytes 884744 | tf_op jit(solution)/shard_map/ppermute | solution.py:19
  145.0 10.1 %collective-permute-done.11 = s16[4,72,512]{2,1,0:T(8,128)(2,1)S(1)} collective-permute-done((s16[4,72,512]{2,1,0:T(8,128)(2,1)S(1)}, s16[4,72,512]{2,1,0:T(8,128)(2,1)S(1)}, u32[]{:S(2)}, u32[]{:S(2)}) %collective-permute-start.11) | collective-permute-done | bytes 294944 | tf_op jit(solution)/shard_map/ppermute | solution.py:19
  164.0 1.9 collective-permute-start.13
  165.9 32.9 %all-gather.3.cloned.1.call-done = bf16[32,32,512]{2,1,0:T(8,128)(2,1)} async-done(((bf16[2,32,512]{2,1,0:T(8,128)(2,1)}), bf16[32,32,512]{2,1,0:T(8,128)(2,1)}) %all-gather.3.cloned.1.call-update) | async-done | bytes 1048592 | tf_op jit(solution)/shard_map/all_gather | solution.py:94
  206.7 2.0 fusion.3
  209.9 14.3 %all-to-all-start.1 = ((s16[16,72,512]{2,1,0:T(8,128)(2,1)}), s16[16,72,512]{2,1,0:T(8,128)(2,1)S(1)}, u32[]{:S(2)}, u32[]{:S(2)}) async-start(s16[16,72,512]{2,1,0:T(8,128)(2,1)} %pad_add_fusion.1), calls=%async_computation.1 | async-start | bytes 2359296 | tf_op jit(solution)/shard_map/all_to_all | solution.py:118
  226.9 2.1 select_bitcast_fusion.1
  229.2 1.6 rev.3
  230.8 2.7 fusion.1
  235.9 5.6 %all-to-all-done.1 = s16[16,72,512]{2,1,0:T(8,128)(2,1)S(1)} async-done(((s16[16,72,512]{2,1,0:T(8,128)(2,1)}), s16[16,72,512]{2,1,0:T(8,128)(2,1)S(1)}, u32[]{:S(2)}, u32[]{:S(2)}) %all-to-all-start.1) | async-done | bytes 1179680 | tf_op jit(solution)/shard_map/all_to_all | solution.py:118
  247.2 5.8 %all-to-all-start.2 = ((s16[32,72,256]{2,1,0:T(8,128)(2,1)}), s16[32,72,256]{2,1,0:T(8,128)(2,1)S(1)}, u32[]{:S(2)}, u32[]{:S(2)}) async-start(s16[32,72,256]{2,1,0:T(8,128)(2,1)} %bitcast.72), calls=%async_computation.2 | async-start | bytes 2359296 | tf_op jit(solution)/shard_map/all_to_all | solution.py:122
  253.1 1.6 slice.404
  254.8 2.3 fusion
  257.2 1.6 slice_select_fusion
  259.0 1.6 copy.117
  260.6 1.6 copy.108
  262.2 1.6 copy.121
  263.7 1.6 copy.124
  265.3 1.6 copy.123
  266.9 1.6 copy.122
  268.5 1.6 copy.125
  273.4 1.9 convolution_multiply_fusion.5
  275.3 1.9 convolution_multiply_fusion.6
  277.2 1.9 convolution_multiply_fusion.1
  279.1 1.9 convolution_multiply_fusion.2
  281.0 1.9 fusion.6
  282.9 2.9 fusion.8
  285.8 1.9 fusion.10
  287.7 2.7 fusion.12
  (217 shorter events, 56.1 us)
Async XLA Ops:
  7.2 12.5 %copy-start.7 = (bf16[256,512]{1,0:T(8,128)(2,1)S(1)}, bf16[256,512]{1,0:T(8,128)(2,1)}, u32[]{:S(2)}) copy-start(bf16[256,512]{1,0:T(8,128)(2,1)} %param.17) | copy-start | bytes 786436
  7.2 12.5 %copy-start.8 = (bf16[256,512]{1,0:T(8,128)(2,1)S(1)}, bf16[256,512]{1,0:T(8,128)(2,1)}, u32[]{:S(2)}) copy-start(bf16[256,512]{1,0:T(8,128)(2,1)} %param.13) | copy-start | bytes 786436
  8.0 16.6 %copy-start.9 = (bf16[512,256]{1,0:T(8,128)(2,1)S(1)}, bf16[512,256]{1,0:T(8,128)(2,1)}, u32[]{:S(2)}) copy-start(bf16[512,256]{1,0:T(8,128)(2,1)} %param.16) | copy-start | bytes 786436
  8.0 16.6 %copy-start.10 = (bf16[512,256]{1,0:T(8,128)(2,1)S(1)}, bf16[512,256]{1,0:T(8,128)(2,1)}, u32[]{:S(2)}) copy-start(bf16[512,256]{1,0:T(8,128)(2,1)} %param.12) | copy-start | bytes 786436
  9.2 38.0 %all-to-all-start = ((bf16[32,2,32,256]{3,2,1,0:T(8,128)(2,1)}), bf16[32,2,32,256]{3,2,1,0:T(8,128)(2,1)S(1)}, u32[]{:S(2)}, u32[]{:S(2)}) async-start(bf16[32,2,32,256]{3,2,1,0:T(8,128)(2,1)} %bitcast.3), calls=%async_computation | async-start | bytes 2097152 | tf_op jit(solution)/shard_map/all_to_all | solution.py:91
  19.6 179.2 %all-gather.3.cloned.1.call-start = ((), (), s32[]{:S(2)}) async-start(), calls=%async_computation.3 | async-start | bytes 1114112 | tf_op jit(solution)/shard_map/all_gather | solution.py:94
  19.8 26.3 %collective-permute-start = (bf16[2,256,512]{2,1,0:T(8,128)(2,1)S(1)}, bf16[2,256,512]{2,1,0:T(8,128)(2,1)}, u32[]{:S(2)}, u32[]{:S(2)}) collective-permute-start(bf16[2,256,512]{2,1,0:T(8,128)(2,1)S(1)} %pad_maximum_fusion.3), channel_id=1, source_target_pairs={{0,16},{16,0},{1,17},{17,1},{2,18},{18,2},{3,19},{19,3},{4,20},{20... | collective-permute-start | bytes 1572872 | tf_op jit(solution)/shard_map/ppermute | solution.py:23
  25.5 113.1 %collective-permute-start.14 = (bf16[2,512,256]{2,1,0:T(8,128)(2,1)}, bf16[2,512,256]{2,1,0:T(8,128)(2,1)}, u32[]{:S(2)}, u32[]{:S(2)}) collective-permute-start(bf16[2,512,256]{2,1,0:T(8,128)(2,1)} %pad_maximum_fusion.4), channel_id=1, source_target_pairs={{0,16},{16,0},{1,17},{17,1},{2,18},{18,2},{3,19},{19,3},{4,20},{20... | collective-permute-start | bytes 1572872 | tf_op jit(solution)/shard_map/ppermute | solution.py:23
  49.9 17.1 %collective-permute-start.3 = (s16[4,72,512]{2,1,0:T(8,128)(2,1)S(1)}, s16[4,72,512]{2,1,0:T(8,128)(2,1)S(1)}, u32[]{:S(2)}, u32[]{:S(2)}) collective-permute-start(s16[4,72,512]{2,1,0:T(8,128)(2,1)S(1)} %pad_add_fusion.4), channel_id=1, source_target_pairs={{0,2},{1,3},{2,4},{3,5},{4,6},{5,7},{6,8},{7,9},{8,10},{9,11},{10,... | collective-permute-start | bytes 884744 | tf_op jit(solution)/shard_map/ppermute | solution.py:19
  53.6 13.8 %collective-permute-start.2 = (s16[4,72,512]{2,1,0:T(8,128)(2,1)S(1)}, s16[4,72,512]{2,1,0:T(8,128)(2,1)S(1)}, u32[]{:S(2)}, u32[]{:S(2)}) collective-permute-start(s16[4,72,512]{2,1,0:T(8,128)(2,1)S(1)} %pad_add_fusion.3), channel_id=1, source_target_pairs={{0,15},{1,0},{2,1},{3,2},{4,3},{5,4},{6,5},{7,6},{8,7},{9,8},{10,9... | collective-permute-start | bytes 884744 | tf_op jit(solution)/shard_map/ppermute | solution.py:19
  62.5 16.3 %collective-permute-start.1 = (s16[4,72,512]{2,1,0:T(8,128)(2,1)S(1)}, s16[4,72,512]{2,1,0:T(8,128)(2,1)}, u32[]{:S(2)}, u32[]{:S(2)}) collective-permute-start(s16[4,72,512]{2,1,0:T(8,128)(2,1)S(1)} %pad_add_fusion.2), channel_id=1, source_target_pairs={{0,1},{1,2},{2,3},{3,4},{4,5},{5,6},{6,7},{7,8},{8,9},{9,10},{10,1... | collective-permute-start | bytes 884744 | tf_op jit(solution)/shard_map/ppermute | solution.py:19
  81.3 54.7 %copy-start.11 = (bf16[32,512]{1,0:T(8,128)(2,1)S(1)}, bf16[32,512]{1,0:T(8,128)(2,1)}, u32[]{:S(2)}) copy-start(bf16[32,512]{1,0:T(8,128)(2,1)} %param.14) | copy-start | bytes 98308
  81.3 54.7 %copy-start.12 = (bf16[32,512]{1,0:T(8,128)(2,1)S(1)}, bf16[32,512]{1,0:T(8,128)(2,1)}, u32[]{:S(2)}) copy-start(bf16[32,512]{1,0:T(8,128)(2,1)} %param.10) | copy-start | bytes 98308
  81.9 19.2 %collective-permute-start.6 = (s16[1,72,512]{2,1,0:T(8,128)(2,1)S(1)}, s16[1,72,512]{2,1,0:T(8,128)(2,1)S(1)}, u32[]{:S(2)}, u32[]{:S(2)}) collective-permute-start(s16[1,72,512]{2,1,0:T(8,128)(2,1)S(1)} %pad_add_fusion.8), channel_id=1, source_target_pairs={{0,8},{1,9},{2,10},{3,11},{4,12},{5,13},{6,14},{7,15},{8,0},{9,1},... | collective-permute-start | bytes 221192 | tf_op jit(solution)/shard_map/ppermute | solution.py:19
  91.6 13.6 %collective-permute-start.5 = (s16[1,72,512]{2,1,0:T(8,128)(2,1)S(1)}, s16[1,72,512]{2,1,0:T(8,128)(2,1)S(1)}, u32[]{:S(2)}, u32[]{:S(2)}) collective-permute-start(s16[1,72,512]{2,1,0:T(8,128)(2,1)S(1)} %pad_add_fusion.7), channel_id=1, source_target_pairs={{0,12},{1,13},{2,14},{3,15},{4,0},{5,1},{6,2},{7,3},{8,4},{9,5},{1... | collective-permute-start | bytes 221192 | tf_op jit(solution)/shard_map/ppermute | solution.py:19
  93.9 14.0 %collective-permute-start.4 = (s16[1,72,512]{2,1,0:T(8,128)(2,1)S(1)}, s16[1,72,512]{2,1,0:T(8,128)(2,1)S(1)}, u32[]{:S(2)}, u32[]{:S(2)}) collective-permute-start(s16[1,72,512]{2,1,0:T(8,128)(2,1)S(1)} %pad_add_fusion.6), channel_id=1, source_target_pairs={{0,4},{1,5},{2,6},{3,7},{4,8},{5,9},{6,10},{7,11},{8,12},{9,13},{1... | collective-permute-start | bytes 221192 | tf_op jit(solution)/shard_map/ppermute | solution.py:19
  111.1 18.3 %collective-permute-start.9 = (s16[1,72,512]{2,1,0:T(8,128)(2,1)S(1)}, s16[1,72,512]{2,1,0:T(8,128)(2,1)S(1)}, u32[]{:S(2)}, u32[]{:S(2)}) collective-permute-start(s16[1,72,512]{2,1,0:T(8,128)(2,1)S(1)} %get-tuple-element.74), channel_id=1, source_target_pairs={{0,8},{1,9},{2,10},{3,11},{4,12},{5,13},{6,14},{7,15},{8,0},{9,1},... | collective-permute-start | bytes 221192 | tf_op jit(solution)/shard_map/ppermute | solution.py:19
  120.2 13.2 %collective-permute-start.8 = (s16[1,72,512]{2,1,0:T(8,128)(2,1)S(1)}, s16[1,72,512]{2,1,0:T(8,128)(2,1)S(1)}, u32[]{:S(2)}, u32[]{:S(2)}) collective-permute-start(s16[1,72,512]{2,1,0:T(8,128)(2,1)S(1)} %get-tuple-element.74), channel_id=1, source_target_pairs={{0,12},{1,13},{2,14},{3,15},{4,0},{5,1},{6,2},{7,3},{8,4},{9,5},{1... | collective-permute-start | bytes 221192 | tf_op jit(solution)/shard_map/ppermute | solution.py:19
  124.3 9.8 %collective-permute-start.7 = (s16[1,72,512]{2,1,0:T(8,128)(2,1)S(1)}, s16[1,72,512]{2,1,0:T(8,128)(2,1)S(1)}, u32[]{:S(2)}, u32[]{:S(2)}) collective-permute-start(s16[1,72,512]{2,1,0:T(8,128)(2,1)S(1)} %get-tuple-element.74), channel_id=1, source_target_pairs={{0,4},{1,5},{2,6},{3,7},{4,8},{5,9},{6,10},{7,11},{8,12},{9,13},{1... | collective-permute-start | bytes 221192 | tf_op jit(solution)/shard_map/ppermute | solution.py:19
  134.1 10.3 %collective-permute-start.10 = (s16[4,72,512]{2,1,0:T(8,128)(2,1)S(1)}, s16[4,72,512]{2,1,0:T(8,128)(2,1)S(1)}, u32[]{:S(2)}, u32[]{:S(2)}) collective-permute-start(s16[4,72,512]{2,1,0:T(8,128)(2,1)S(1)} %pad_add_fusion.5), channel_id=1, source_target_pairs={{0,1},{1,2},{2,3},{3,4},{4,5},{5,6},{6,7},{7,8},{8,9},{9,10},{10,1... | collective-permute-start | bytes 884744 | tf_op jit(solution)/shard_map/ppermute | solution.py:19
  136.7 18.4 %collective-permute-start.11 = (s16[4,72,512]{2,1,0:T(8,128)(2,1)S(1)}, s16[4,72,512]{2,1,0:T(8,128)(2,1)S(1)}, u32[]{:S(2)}, u32[]{:S(2)}) collective-permute-start(s16[4,72,512]{2,1,0:T(8,128)(2,1)S(1)} %pad_add_fusion.5), channel_id=1, source_target_pairs={{0,2},{1,3},{2,4},{3,5},{4,6},{5,7},{6,8},{7,9},{8,10},{9,11},{10,... | collective-permute-start | bytes 884744 | tf_op jit(solution)/shard_map/ppermute | solution.py:19
  139.7 16.0 %collective-permute-start.12 = (s16[4,72,512]{2,1,0:T(8,128)(2,1)S(1)}, s16[4,72,512]{2,1,0:T(8,128)(2,1)S(1)}, u32[]{:S(2)}, u32[]{:S(2)}) collective-permute-start(s16[4,72,512]{2,1,0:T(8,128)(2,1)S(1)} %pad_add_fusion.5), channel_id=1, source_target_pairs={{0,15},{1,0},{2,1},{3,2},{4,3},{5,4},{6,5},{7,6},{8,7},{9,8},{10,9... | collective-permute-start | bytes 884744 | tf_op jit(solution)/shard_map/ppermute | solution.py:19
  164.0 62.9 %collective-permute-start.13 = (s16[16,72,512]{2,1,0:T(8,128)(2,1)}, s16[16,72,512]{2,1,0:T(8,128)(2,1)}, u32[]{:S(2)}, u32[]{:S(2)}) collective-permute-start(s16[16,72,512]{2,1,0:T(8,128)(2,1)} %slice_dynamic-update-slice_fusion), channel_id=1, source_target_pairs={{0,16},{16,0},{1,17},{17,1},{2,18},{18,2},{3,19},{19,3},{4,20},{20... | collective-permute-start | bytes 3538952 | tf_op jit(solution)/shard_map/ppermute | solution.py:23
  208.8 15.4 %copy-start.17 = (s32[1024]{0:T(1024)S(1)}, s32[1024]{0:T(1024)}, u32[]{:S(2)}) copy-start(s32[1024]{0:T(1024)} %param.9) | copy-start | bytes 12292
  209.9 31.6 %all-to-all-start.1 = ((s16[16,72,512]{2,1,0:T(8,128)(2,1)}), s16[16,72,512]{2,1,0:T(8,128)(2,1)S(1)}, u32[]{:S(2)}, u32[]{:S(2)}) async-start(s16[16,72,512]{2,1,0:T(8,128)(2,1)} %pad_add_fusion.1), calls=%async_computation.1 | async-start | bytes 2359296 | tf_op jit(solution)/shard_map/all_to_all | solution.py:118
  245.5 7.6 %copy-start.18 = (s16[2,16,1]{1,0,2:T(2,128)(2,1)S(1)}, s16[2,16,1]{1,0,2:T(2,128)(2,1)}, u32[]{:S(2)}) copy-start(s16[2,16,1]{1,0,2:T(2,128)(2,1)} %stack.221) | copy-start | bytes 196
  245.5 7.6 %copy-start.19 = (s16[2,16,1]{1,0,2:T(2,128)(2,1)S(1)}, s16[2,16,1]{1,0,2:T(2,128)(2,1)}, u32[]{:S(2)}) copy-start(s16[2,16,1]{1,0,2:T(2,128)(2,1)} %stack.220) | copy-start | bytes 196
  247.2 24.2 %all-to-all-start.2 = ((s16[32,72,256]{2,1,0:T(8,128)(2,1)}), s16[32,72,256]{2,1,0:T(8,128)(2,1)S(1)}, u32[]{:S(2)}, u32[]{:S(2)}) async-start(s16[32,72,256]{2,1,0:T(8,128)(2,1)} %bitcast.72), calls=%async_computation.2 | async-start | bytes 2359296 | tf_op jit(solution)/shard_map/all_to_all | solution.py:122
  254.8 2.3 copy-start.13
  254.8 2.3 copy-start.14
  254.8 2.3 copy-start.15
  254.8 2.3 copy-start.16
  273.4 1.9 copy-start
  275.3 1.9 copy-start.1
  277.2 1.9 copy-start.2
  279.1 1.9 copy-start.5
  281.0 1.9 copy-start.3
  282.9 2.9 copy-start.6
  285.8 1.9 copy-start.4
Sparse Core Ops, SparseCore 0:
  136.8 61.9 all-gather.2
where the time goes:
time: 299 us; the launch traced here: 297 us
  starting transfers between devices  97.5 us (33%)
  waiting for transfers between devices  89.7 us (30%)
  local copies, waits for them, and re-layouts  48.1 us (16%)
  other arithmetic  27.5 us (9%)
  matrix products  19.4 us (6%)
  between operations  15 us (5%)
    ppermute x12, starting transfers between devices, shift(): return lax.ppermute(x, Z, [(i, (i + by) % NZ) for i in range(NZ)])  58.2 us
    all_gather x1, waiting for transfers between devices, per_device(): inputs = lax.all_gather(jnp.stack([qx, ox])[None], Z, axis=0, tiled=True)  32.9 us
    ppermute x12, waiting for transfers between devices, shift(): return lax.ppermute(x, Z, [(i, (i + by) % NZ) for i in range(NZ)])  31.4 us
    ppermute x3, waiting for transfers between devices, swap_half(): return lax.ppermute(x, 'xh', [(0, 1), (1, 0)])  18.6 us
    dot_general x8, matrix products, correct(): lax.dot_general(grad_rows, act_rot, (((0,), (0,)), ((), ())), precision=l...  16.8 us
    all_to_all x1, starting transfers between devices, per_device(): lax.all_to_all(act_words, ROW, split_axis=0, concat_axis=0, tiled=True)  14.3 us
    select_n x8, local copies, waits for them, and re-layouts, correct(): grad_rows = jnp.where((seq_ids == seq)[:, None], grad_rot, 0.0)  11.3 us
    all_to_all x1, starting transfers between devices, per_device(): got = lax.all_to_all(sent, PLANE, split_axis=0, concat_axis=0, tiled=True)  10.5 us
  transfers between devices with their start and end apart: 19, of which 11 were waited for; matrix products, arithmetic and copies ran while one was open for 23% of the time, Pallas kernels for 0%

commit v1 on v0

--- a/solution.py
+++ b/solution.py
@@ -91,7 +91,9 @@
     got = lax.all_to_all(sent, PLANE, split_axis=0, concat_axis=0, tiled=True)
     grad_basis = jnp.stack([qb, ob])
     grad_other = swap_half(grad_basis)
-    inputs = lax.all_gather(jnp.stack([qx, ox])[None], Z, axis=0, tiled=True)
+    inputs = jnp.concatenate(
+        lax.all_to_all(jnp.stack([jnp.stack([qx, ox])[None]] * lax.axis_size(Z)), Z, 0, 0), axis=0
+    )
     act_basis = jnp.stack([qa, oa])
     act_other = swap_half(act_basis)
     got = got.reshape(2, 16, 2, 32, 256)

time: 299 us -> 303 us (1.013)
  between operations: 15 us -> 1.63 us
  starting transfers between devices: 97.5 us -> 106 us
  waiting for transfers between devices: 89.7 us -> 94.1 us
  local copies, waits for them, and re-layouts: 48.1 us -> 51.4 us
    ppermute x12, waiting for transfers between devices: 31.4 us -> 66.4 us  [shift(): return lax.ppermute(x, Z, [(i, (i + by) % NZ) for i in range(NZ)])]
    all_gather x1 -> x0, waiting for transfers between devices: 32.9 us -> none  [per_device(): inputs = lax.all_gather(jnp.stack([qx, ox])[None], Z, axis=0, tiled=True)]
    all_to_all x0 -> x1, starting transfers between devices: none -> 12.9 us  [per_device(): lax.all_to_all(jnp.stack([jnp.stack([qx, ox])[None]] * lax.axis_size(Z)),...]
    ppermute x12, starting transfers between devices: 58.2 us -> 54.8 us  [shift(): return lax.ppermute(x, Z, [(i, (i + by) % NZ) for i in range(NZ)])]
    unnamed x54 -> x56, local copies, waits for them, and re-layouts: 8.98 us -> 8.98 us
  transfers between devices with their start and end apart: 19 -> 19, of which waited for: 11 -> 9; matrix products, arithmetic and copies ran while one was open for 23% -> 24% of each run, Pallas kernels for 0% -> 0%
where the time goes in v1:
time: 303 us; the launch traced here: 299 us
  starting transfers between devices  106 us (35%)
  waiting for transfers between devices  94.1 us (31%)
  local copies, waits for them, and re-layouts  51.4 us (17%)
  other arithmetic  26.6 us (9%)
  matrix products  19.3 us (6%)
    ppermute x12, waiting for transfers between devices, shift(): return lax.ppermute(x, Z, [(i, (i + by) % NZ) for i in range(NZ)])  66.4 us
    ppermute x12, starting transfers between devices, shift(): return lax.ppermute(x, Z, [(i, (i + by) % NZ) for i in range(NZ)])  54.8 us
    ppermute x3, waiting for transfers between devices, swap_half(): return lax.ppermute(x, 'xh', [(0, 1), (1, 0)])  18.6 us
    dot_general x8, matrix products, correct(): lax.dot_general(grad_rows, act_rot, (((0,), (0,)), ((), ())), precision=l...  16.8 us
    all_to_all x1, starting transfers between devices, per_device(): lax.all_to_all(jnp.stack([jnp.stack([qx, ox])[None]] * lax.axis_size(Z)),...  12.9 us
    all_to_all x1, starting transfers between devices, per_device(): lax.all_to_all(act_words, ROW, split_axis=0, concat_axis=0, tiled=True)  11.4 us
    select_n x8, local copies, waits for them, and re-layouts, correct(): grad_rows = jnp.where((seq_ids == seq)[:, None], grad_rot, 0.0)  11.3 us
    all_to_all x1, starting transfers between devices, per_device(): got = lax.all_to_all(sent, PLANE, split_axis=0, concat_axis=0, tiled=True)  10.6 us
  transfers between devices with their start and end apart: 19, of which 9 were waited for; matrix products, arithmetic and copies ran while one was open for 24% of the time, Pallas kernels for 0%

profile of v1, /device:TPU:1, one launch (start us, length us, event | category | flops | bytes accessed | tf_op | source)
XLA Modules:
  0.0 299.1 jit_solution(10132512968905502537)
XLA Ops:
  2.6 10.6 %all-to-all-start = ((bf16[32,2,32,256]{3,2,1,0:T(8,128)(2,1)}), bf16[32,2,32,256]{3,2,1,0:T(8,128)(2,1)S(1)}, u32[]{:S(2)}, u32[]{:S(2)}) async-start(bf16[32,2,32,256]{3,2,1,0:T(8,128)(2,1)} %bitcast.3), calls=%async_computation | async-start | bytes 2097152 | tf_op jit(solution)/shard_map/all_to_all | solution.py:91
  13.3 4.9 %collective-permute-start = (bf16[2,256,512]{2,1,0:T(8,128)(2,1)S(1)}, bf16[2,256,512]{2,1,0:T(8,128)(2,1)}, u32[]{:S(2)}, u32[]{:S(2)}) collective-permute-start(bf16[2,256,512]{2,1,0:T(8,128)(2,1)S(1)} %pad_maximum_fusion.3), channel_id=1, source_target_pairs={{0,16},{16,0},{1,17},{17,1},{2,18},{18,2},{3,19},{19,3},{4,20},{20... | collective-permute-start | bytes 1572872 | tf_op jit(solution)/shard_map/ppermute | solution.py:23
  19.1 1.9 collective-permute-start.14
  21.0 18.6 %collective-permute-done = bf16[2,256,512]{2,1,0:T(8,128)(2,1)} collective-permute-done((bf16[2,256,512]{2,1,0:T(8,128)(2,1)S(1)}, bf16[2,256,512]{2,1,0:T(8,128)(2,1)}, u32[]{:S(2)}, u32[]{:S(2)}) %collective-permute-start) | collective-permute-done | bytes 524320 | tf_op jit(solution)/shard_map/ppermute | solution.py:23
  41.9 12.9 %all-to-all-start.1 = ((bf16[16,1,2,32,512]{4,3,2,1,0:T(8,128)(2,1)}), bf16[16,1,2,32,512]{4,3,2,1,0:T(8,128)(2,1)S(1)}, u32[]{:S(2)}, u32[]{:S(2)}) async-start(bf16[16,1,2,32,512]{4,3,2,1,0:T(8,128)(2,1)} %stack.229), calls=%async_computation.1 | async-start | bytes 2097152 | tf_op jit(solution)/shard_map/all_to_all | solution.py:95
  57.5 4.2 %collective-permute-start.3 = (s16[4,72,512]{2,1,0:T(8,128)(2,1)S(1)}, s16[4,72,512]{2,1,0:T(8,128)(2,1)}, u32[]{:S(2)}, u32[]{:S(2)}) collective-permute-start(s16[4,72,512]{2,1,0:T(8,128)(2,1)S(1)} %pad_add_fusion.4), channel_id=1, source_target_pairs={{0,2},{1,3},{2,4},{3,5},{4,6},{5,7},{6,8},{7,9},{8,10},{9,11},{10,... | collective-permute-start | bytes 884744 | tf_op jit(solution)/shard_map/ppermute | solution.py:19
  62.4 3.4 %collective-permute-start.2 = (s16[4,72,512]{2,1,0:T(8,128)(2,1)S(1)}, s16[4,72,512]{2,1,0:T(8,128)(2,1)}, u32[]{:S(2)}, u32[]{:S(2)}) collective-permute-start(s16[4,72,512]{2,1,0:T(8,128)(2,1)S(1)} %pad_add_fusion.3), channel_id=1, source_target_pairs={{0,15},{1,0},{2,1},{3,2},{4,3},{5,4},{6,5},{7,6},{8,7},{9,8},{10,9... | collective-permute-start | bytes 884744 | tf_op jit(solution)/shard_map/ppermute | solution.py:19
  66.6 1.9 collective-permute-start.1
  68.5 43.1 %collective-permute-done.3 = s16[4,72,512]{2,1,0:T(8,128)(2,1)} collective-permute-done((s16[4,72,512]{2,1,0:T(8,128)(2,1)S(1)}, s16[4,72,512]{2,1,0:T(8,128)(2,1)}, u32[]{:S(2)}, u32[]{:S(2)}) %collective-permute-start.3) | collective-permute-done | bytes 294944 | tf_op jit(solution)/shard_map/ppermute | solution.py:19
  113.9 8.0 %collective-permute-done.1 = s16[4,72,512]{2,1,0:T(8,128)(2,1)} collective-permute-done((s16[4,72,512]{2,1,0:T(8,128)(2,1)S(1)}, s16[4,72,512]{2,1,0:T(8,128)(2,1)}, u32[]{:S(2)}, u32[]{:S(2)}) %collective-permute-start.1) | collective-permute-done | bytes 294944 | tf_op jit(solution)/shard_map/ppermute | solution.py:19
  126.9 10.6 %collective-permute-start.6 = (s16[1,72,512]{2,1,0:T(8,128)(2,1)S(1)}, s16[1,72,512]{2,1,0:T(8,128)(2,1)S(1)}, u32[]{:S(2)}, u32[]{:S(2)}) collective-permute-start(s16[1,72,512]{2,1,0:T(8,128)(2,1)S(1)} %pad_add_fusion.8), channel_id=1, source_target_pairs={{0,8},{1,9},{2,10},{3,11},{4,12},{5,13},{6,14},{7,15},{8,0},{9,1},... | collective-permute-start | bytes 221192 | tf_op jit(solution)/shard_map/ppermute | solution.py:19
  137.8 1.9 collective-permute-start.5
  140.1 7.3 %collective-permute-start.4 = (s16[1,72,512]{2,1,0:T(8,128)(2,1)S(1)}, s16[1,72,512]{2,1,0:T(8,128)(2,1)S(1)}, u32[]{:S(2)}, u32[]{:S(2)}) collective-permute-start(s16[1,72,512]{2,1,0:T(8,128)(2,1)S(1)} %pad_add_fusion.6), channel_id=1, source_target_pairs={{0,4},{1,5},{2,6},{3,7},{4,8},{5,9},{6,10},{7,11},{8,12},{9,13},{1... | collective-permute-start | bytes 221192 | tf_op jit(solution)/shard_map/ppermute | solution.py:19
  149.3 1.9 collective-permute-done.5
  156.8 8.0 %collective-permute-start.9 = (s16[1,72,512]{2,1,0:T(8,128)(2,1)S(1)}, s16[1,72,512]{2,1,0:T(8,128)(2,1)S(1)}, u32[]{:S(2)}, u32[]{:S(2)}) collective-permute-start(s16[1,72,512]{2,1,0:T(8,128)(2,1)S(1)} %get-tuple-element.74), channel_id=1, source_target_pairs={{0,8},{1,9},{2,10},{3,11},{4,12},{5,13},{6,14},{7,15},{8,0},{9,1},... | collective-permute-start | bytes 221192 | tf_op jit(solution)/shard_map/ppermute | solution.py:19
  164.7 5.9 %collective-permute-start.8 = (s16[1,72,512]{2,1,0:T(8,128)(2,1)S(1)}, s16[1,72,512]{2,1,0:T(8,128)(2,1)S(1)}, u32[]{:S(2)}, u32[]{:S(2)}) collective-permute-start(s16[1,72,512]{2,1,0:T(8,128)(2,1)S(1)} %get-tuple-element.74), channel_id=1, source_target_pairs={{0,12},{1,13},{2,14},{3,15},{4,0},{5,1},{6,2},{7,3},{8,4},{9,5},{1... | collective-permute-start | bytes 221192 | tf_op jit(solution)/shard_map/ppermute | solution.py:19
  170.6 3.3 %collective-permute-start.7 = (s16[1,72,512]{2,1,0:T(8,128)(2,1)S(1)}, s16[1,72,512]{2,1,0:T(8,128)(2,1)S(1)}, u32[]{:S(2)}, u32[]{:S(2)}) collective-permute-start(s16[1,72,512]{2,1,0:T(8,128)(2,1)S(1)} %get-tuple-element.74), channel_id=1, source_target_pairs={{0,4},{1,5},{2,6},{3,7},{4,8},{5,9},{6,10},{7,11},{8,12},{9,13},{1... | collective-permute-start | bytes 221192 | tf_op jit(solution)/shard_map/ppermute | solution.py:19
  173.9 6.2 %collective-permute-done.8 = s16[1,72,512]{2,1,0:T(8,128)(2,1)S(1)} collective-permute-done((s16[1,72,512]{2,1,0:T(8,128)(2,1)S(1)}, s16[1,72,512]{2,1,0:T(8,128)(2,1)S(1)}, u32[]{:S(2)}, u32[]{:S(2)}) %collective-permute-start.8) | collective-permute-done | bytes 73760 | tf_op jit(solution)/shard_map/ppermute | solution.py:19
  180.2 1.9 collective-permute-start.10
  182.1 1.9 collective-permute-start.11
  185.2 4.6 %collective-permute-start.12 = (s16[4,72,512]{2,1,0:T(8,128)(2,1)S(1)}, s16[4,72,512]{2,1,0:T(8,128)(2,1)S(1)}, u32[]{:S(2)}, u32[]{:S(2)}) collective-permute-start(s16[4,72,512]{2,1,0:T(8,128)(2,1)S(1)} %pad_add_fusion.5), channel_id=1, source_target_pairs={{0,15},{1,0},{2,1},{3,2},{4,3},{5,4},{6,5},{7,6},{8,7},{9,8},{10,9... | collective-permute-start | bytes 884744 | tf_op jit(solution)/shard_map/ppermute | solution.py:19
  190.4 6.7 %collective-permute-done.11 = s16[4,72,512]{2,1,0:T(8,128)(2,1)S(1)} collective-permute-done((s16[4,72,512]{2,1,0:T(8,128)(2,1)S(1)}, s16[4,72,512]{2,1,0:T(8,128)(2,1)S(1)}, u32[]{:S(2)}, u32[]{:S(2)}) %collective-permute-start.11) | collective-permute-done | bytes 294944 | tf_op jit(solution)/shard_map/ppermute | solution.py:19
  206.0 1.9 collective-permute-start.13
  212.9 1.6 copy.85
  214.7 2.0 fusion.3
  217.9 11.4 %all-to-all-start.2 = ((s16[16,72,512]{2,1,0:T(8,128)(2,1)}), s16[16,72,512]{2,1,0:T(8,128)(2,1)S(1)}, u32[]{:S(2)}, u32[]{:S(2)}) async-start(s16[16,72,512]{2,1,0:T(8,128)(2,1)} %pad_add_fusion.1), calls=%async_computation.2 | async-start | bytes 2359296 | tf_op jit(solution)/shard_map/all_to_all | solution.py:120
  232.0 2.1 select_bitcast_fusion.1
  234.3 1.6 rev.3
  235.9 2.7 fusion.1
  241.0 7.5 %all-to-all-done.2 = s16[16,72,512]{2,1,0:T(8,128)(2,1)S(1)} async-done(((s16[16,72,512]{2,1,0:T(8,128)(2,1)}), s16[16,72,512]{2,1,0:T(8,128)(2,1)S(1)}, u32[]{:S(2)}, u32[]{:S(2)}) %all-to-all-start.2) | async-done | bytes 1179680 | tf_op jit(solution)/shard_map/all_to_all | solution.py:120
  254.3 7.5 %all-to-all-start.3 = ((s16[32,72,256]{2,1,0:T(8,128)(2,1)}), s16[32,72,256]{2,1,0:T(8,128)(2,1)S(1)}, u32[]{:S(2)}, u32[]{:S(2)}) async-start(s16[32,72,256]{2,1,0:T(8,128)(2,1)} %bitcast.72), calls=%async_computation.3 | async-start | bytes 2359296 | tf_op jit(solution)/shard_map/all_to_all | solution.py:124
  261.8 1.6 slice.404
  263.6 2.3 fusion
  267.5 1.6 copy.91
  269.1 1.6 copy.82
  270.7 1.6 copy.95
  272.3 1.6 copy.98
  273.8 1.6 copy.97
  275.4 1.6 copy.96
  277.0 1.6 copy.99
  282.2 1.9 convolution_multiply_fusion.5
  284.1 1.9 convolution_multiply_fusion.6
  286.0 1.9 convolution_multiply_fusion.1
  287.9 1.9 convolution_multiply_fusion.2
  289.8 1.9 fusion.6
  291.7 2.9 fusion.8
  294.6 1.9 fusion.10
  296.4 2.7 fusion.12
  (219 shorter events, 57.8 us)
Async XLA Ops:
  0.6 12.6 %copy-start.7 = (bf16[256,512]{1,0:T(8,128)(2,1)S(1)}, bf16[256,512]{1,0:T(8,128)(2,1)}, u32[]{:S(2)}) copy-start(bf16[256,512]{1,0:T(8,128)(2,1)} %param.17) | copy-start | bytes 786436
  0.6 12.6 %copy-start.8 = (bf16[256,512]{1,0:T(8,128)(2,1)S(1)}, bf16[256,512]{1,0:T(8,128)(2,1)}, u32[]{:S(2)}) copy-start(bf16[256,512]{1,0:T(8,128)(2,1)} %param.13) | copy-start | bytes 786436
  1.5 16.7 %copy-start.9 = (bf16[512,256]{1,0:T(8,128)(2,1)S(1)}, bf16[512,256]{1,0:T(8,128)(2,1)}, u32[]{:S(2)}) copy-start(bf16[512,256]{1,0:T(8,128)(2,1)} %param.16) | copy-start | bytes 786436
  1.5 16.7 %copy-start.10 = (bf16[512,256]{1,0:T(8,128)(2,1)S(1)}, bf16[512,256]{1,0:T(8,128)(2,1)}, u32[]{:S(2)}) copy-start(bf16[512,256]{1,0:T(8,128)(2,1)} %param.12) | copy-start | bytes 786436
  2.6 18.4 %copy-start.12 = (bf16[32,512]{1,0:T(8,128)(2,1)S(1)}, bf16[32,512]{1,0:T(8,128)(2,1)}, u32[]{:S(2)}) copy-start(bf16[32,512]{1,0:T(8,128)(2,1)} %param.14) | copy-start | bytes 98308
  2.6 18.4 %copy-start.13 = (bf16[32,512]{1,0:T(8,128)(2,1)S(1)}, bf16[32,512]{1,0:T(8,128)(2,1)}, u32[]{:S(2)}) copy-start(bf16[32,512]{1,0:T(8,128)(2,1)} %param.10) | copy-start | bytes 98308
  2.6 38.2 %all-to-all-start = ((bf16[32,2,32,256]{3,2,1,0:T(8,128)(2,1)}), bf16[32,2,32,256]{3,2,1,0:T(8,128)(2,1)S(1)}, u32[]{:S(2)}, u32[]{:S(2)}) async-start(bf16[32,2,32,256]{3,2,1,0:T(8,128)(2,1)} %bitcast.3), calls=%async_computation | async-start | bytes 2097152 | tf_op jit(solution)/shard_map/all_to_all | solution.py:91
  13.3 26.4 %collective-permute-start = (bf16[2,256,512]{2,1,0:T(8,128)(2,1)S(1)}, bf16[2,256,512]{2,1,0:T(8,128)(2,1)}, u32[]{:S(2)}, u32[]{:S(2)}) collective-permute-start(bf16[2,256,512]{2,1,0:T(8,128)(2,1)S(1)} %pad_maximum_fusion.3), channel_id=1, source_target_pairs={{0,16},{16,0},{1,17},{17,1},{2,18},{18,2},{3,19},{19,3},{4,20},{20... | collective-permute-start | bytes 1572872 | tf_op jit(solution)/shard_map/ppermute | solution.py:23
  19.1 165.0 %collective-permute-start.14 = (bf16[2,512,256]{2,1,0:T(8,128)(2,1)}, bf16[2,512,256]{2,1,0:T(8,128)(2,1)}, u32[]{:S(2)}, u32[]{:S(2)}) collective-permute-start(bf16[2,512,256]{2,1,0:T(8,128)(2,1)} %pad_maximum_fusion.4), channel_id=1, source_target_pairs={{0,16},{16,0},{1,17},{17,1},{2,18},{18,2},{3,19},{19,3},{4,20},{20... | collective-permute-start | bytes 1572872 | tf_op jit(solution)/shard_map/ppermute | solution.py:23
  41.9 166.1 %all-to-all-start.1 = ((bf16[16,1,2,32,512]{4,3,2,1,0:T(8,128)(2,1)}), bf16[16,1,2,32,512]{4,3,2,1,0:T(8,128)(2,1)S(1)}, u32[]{:S(2)}, u32[]{:S(2)}) async-start(bf16[16,1,2,32,512]{4,3,2,1,0:T(8,128)(2,1)} %stack.229), calls=%async_computation.1 | async-start | bytes 2097152 | tf_op jit(solution)/shard_map/all_to_all | solution.py:95
  57.5 54.1 %collective-permute-start.3 = (s16[4,72,512]{2,1,0:T(8,128)(2,1)S(1)}, s16[4,72,512]{2,1,0:T(8,128)(2,1)}, u32[]{:S(2)}, u32[]{:S(2)}) collective-permute-start(s16[4,72,512]{2,1,0:T(8,128)(2,1)S(1)} %pad_add_fusion.4), channel_id=1, source_target_pairs={{0,2},{1,3},{2,4},{3,5},{4,6},{5,7},{6,8},{7,9},{8,10},{9,11},{10,... | collective-permute-start | bytes 884744 | tf_op jit(solution)/shard_map/ppermute | solution.py:19
  62.4 50.3 %collective-permute-start.2 = (s16[4,72,512]{2,1,0:T(8,128)(2,1)S(1)}, s16[4,72,512]{2,1,0:T(8,128)(2,1)}, u32[]{:S(2)}, u32[]{:S(2)}) collective-permute-start(s16[4,72,512]{2,1,0:T(8,128)(2,1)S(1)} %pad_add_fusion.3), channel_id=1, source_target_pairs={{0,15},{1,0},{2,1},{3,2},{4,3},{5,4},{6,5},{7,6},{8,7},{9,8},{10,9... | collective-permute-start | bytes 884744 | tf_op jit(solution)/shard_map/ppermute | solution.py:19
  66.6 55.3 %collective-permute-start.1 = (s16[4,72,512]{2,1,0:T(8,128)(2,1)S(1)}, s16[4,72,512]{2,1,0:T(8,128)(2,1)}, u32[]{:S(2)}, u32[]{:S(2)}) collective-permute-start(s16[4,72,512]{2,1,0:T(8,128)(2,1)S(1)} %pad_add_fusion.2), channel_id=1, source_target_pairs={{0,1},{1,2},{2,3},{3,4},{4,5},{5,6},{6,7},{7,8},{8,9},{9,10},{10,1... | collective-permute-start | bytes 884744 | tf_op jit(solution)/shard_map/ppermute | solution.py:19
  126.3 57.8 %copy-start.11 = (bf16[512,256]{1,0:T(8,128)(2,1)S(1)}, bf16[512,256]{1,0:T(8,128)(2,1)}, u32[]{:S(2)}) copy-start(bf16[512,256]{1,0:T(8,128)(2,1)} %param.12) | copy-start | bytes 786436
  126.9 20.5 %collective-permute-start.6 = (s16[1,72,512]{2,1,0:T(8,128)(2,1)S(1)}, s16[1,72,512]{2,1,0:T(8,128)(2,1)S(1)}, u32[]{:S(2)}, u32[]{:S(2)}) collective-permute-start(s16[1,72,512]{2,1,0:T(8,128)(2,1)S(1)} %pad_add_fusion.8), channel_id=1, source_target_pairs={{0,8},{1,9},{2,10},{3,11},{4,12},{5,13},{6,14},{7,15},{8,0},{9,1},... | collective-permute-start | bytes 221192 | tf_op jit(solution)/shard_map/ppermute | solution.py:19
  137.8 13.3 %collective-permute-start.5 = (s16[1,72,512]{2,1,0:T(8,128)(2,1)S(1)}, s16[1,72,512]{2,1,0:T(8,128)(2,1)S(1)}, u32[]{:S(2)}, u32[]{:S(2)}) collective-permute-start(s16[1,72,512]{2,1,0:T(8,128)(2,1)S(1)} %pad_add_fusion.7), channel_id=1, source_target_pairs={{0,12},{1,13},{2,14},{3,15},{4,0},{5,1},{6,2},{7,3},{8,4},{9,5},{1... | collective-permute-start | bytes 221192 | tf_op jit(solution)/shard_map/ppermute | solution.py:19
  140.1 13.5 %collective-permute-start.4 = (s16[1,72,512]{2,1,0:T(8,128)(2,1)S(1)}, s16[1,72,512]{2,1,0:T(8,128)(2,1)S(1)}, u32[]{:S(2)}, u32[]{:S(2)}) collective-permute-start(s16[1,72,512]{2,1,0:T(8,128)(2,1)S(1)} %pad_add_fusion.6), channel_id=1, source_target_pairs={{0,4},{1,5},{2,6},{3,7},{4,8},{5,9},{6,10},{7,11},{8,12},{9,13},{1... | collective-permute-start | bytes 221192 | tf_op jit(solution)/shard_map/ppermute | solution.py:19
  156.8 17.2 %collective-permute-start.9 = (s16[1,72,512]{2,1,0:T(8,128)(2,1)S(1)}, s16[1,72,512]{2,1,0:T(8,128)(2,1)S(1)}, u32[]{:S(2)}, u32[]{:S(2)}) collective-permute-start(s16[1,72,512]{2,1,0:T(8,128)(2,1)S(1)} %get-tuple-element.74), channel_id=1, source_target_pairs={{0,8},{1,9},{2,10},{3,11},{4,12},{5,13},{6,14},{7,15},{8,0},{9,1},... | collective-permute-start | bytes 221192 | tf_op jit(solution)/shard_map/ppermute | solution.py:19
  164.7 15.4 %collective-permute-start.8 = (s16[1,72,512]{2,1,0:T(8,128)(2,1)S(1)}, s16[1,72,512]{2,1,0:T(8,128)(2,1)S(1)}, u32[]{:S(2)}, u32[]{:S(2)}) collective-permute-start(s16[1,72,512]{2,1,0:T(8,128)(2,1)S(1)} %get-tuple-element.74), channel_id=1, source_target_pairs={{0,12},{1,13},{2,14},{3,15},{4,0},{5,1},{6,2},{7,3},{8,4},{9,5},{1... | collective-permute-start | bytes 221192 | tf_op jit(solution)/shard_map/ppermute | solution.py:19
  170.6 9.5 %collective-permute-start.7 = (s16[1,72,512]{2,1,0:T(8,128)(2,1)S(1)}, s16[1,72,512]{2,1,0:T(8,128)(2,1)S(1)}, u32[]{:S(2)}, u32[]{:S(2)}) collective-permute-start(s16[1,72,512]{2,1,0:T(8,128)(2,1)S(1)} %get-tuple-element.74), channel_id=1, source_target_pairs={{0,4},{1,5},{2,6},{3,7},{4,8},{5,9},{6,10},{7,11},{8,12},{9,13},{1... | collective-permute-start | bytes 221192 | tf_op jit(solution)/shard_map/ppermute | solution.py:19
  180.2 9.6 %collective-permute-start.10 = (s16[4,72,512]{2,1,0:T(8,128)(2,1)S(1)}, s16[4,72,512]{2,1,0:T(8,128)(2,1)S(1)}, u32[]{:S(2)}, u32[]{:S(2)}) collective-permute-start(s16[4,72,512]{2,1,0:T(8,128)(2,1)S(1)} %pad_add_fusion.5), channel_id=1, source_target_pairs={{0,1},{1,2},{2,3},{3,4},{4,5},{5,6},{6,7},{7,8},{8,9},{9,10},{10,1... | collective-permute-start | bytes 884744 | tf_op jit(solution)/shard_map/ppermute | solution.py:19
  182.1 15.0 %collective-permute-start.11 = (s16[4,72,512]{2,1,0:T(8,128)(2,1)S(1)}, s16[4,72,512]{2,1,0:T(8,128)(2,1)S(1)}, u32[]{:S(2)}, u32[]{:S(2)}) collective-permute-start(s16[4,72,512]{2,1,0:T(8,128)(2,1)S(1)} %pad_add_fusion.5), channel_id=1, source_target_pairs={{0,2},{1,3},{2,4},{3,5},{4,6},{5,7},{6,8},{7,9},{8,10},{9,11},{10,... | collective-permute-start | bytes 884744 | tf_op jit(solution)/shard_map/ppermute | solution.py:19
  185.2 12.6 %collective-permute-start.12 = (s16[4,72,512]{2,1,0:T(8,128)(2,1)S(1)}, s16[4,72,512]{2,1,0:T(8,128)(2,1)S(1)}, u32[]{:S(2)}, u32[]{:S(2)}) collective-permute-start(s16[4,72,512]{2,1,0:T(8,128)(2,1)S(1)} %pad_add_fusion.5), channel_id=1, source_target_pairs={{0,15},{1,0},{2,1},{3,2},{4,3},{5,4},{6,5},{7,6},{8,7},{9,8},{10,9... | collective-permute-start | bytes 884744 | tf_op jit(solution)/shard_map/ppermute | solution.py:19
  206.0 26.0 %collective-permute-start.13 = (s16[16,72,512]{2,1,0:T(8,128)(2,1)}, s16[16,72,512]{2,1,0:T(8,128)(2,1)}, u32[]{:S(2)}, u32[]{:S(2)}) collective-permute-start(s16[16,72,512]{2,1,0:T(8,128)(2,1)} %slice_dynamic-update-slice_fusion), channel_id=1, source_target_pairs={{0,16},{16,0},{1,17},{17,1},{2,18},{18,2},{3,19},{19,3},{4,20},{20... | collective-permute-start | bytes 3538952 | tf_op jit(solution)/shard_map/ppermute | solution.py:23
  216.8 12.5 %copy-start.18 = (s32[1024]{0:T(1024)S(1)}, s32[1024]{0:T(1024)}, u32[]{:S(2)}) copy-start(s32[1024]{0:T(1024)} %param.9) | copy-start | bytes 12292
  217.9 30.6 %all-to-all-start.2 = ((s16[16,72,512]{2,1,0:T(8,128)(2,1)}), s16[16,72,512]{2,1,0:T(8,128)(2,1)S(1)}, u32[]{:S(2)}, u32[]{:S(2)}) async-start(s16[16,72,512]{2,1,0:T(8,128)(2,1)} %pad_add_fusion.1), calls=%async_computation.2 | async-start | bytes 2359296 | tf_op jit(solution)/shard_map/all_to_all | solution.py:120
  252.5 9.3 %copy-start.19 = (s16[2,16,1]{1,0,2:T(2,128)(2,1)S(1)}, s16[2,16,1]{1,0,2:T(2,128)(2,1)}, u32[]{:S(2)}) copy-start(s16[2,16,1]{1,0,2:T(2,128)(2,1)} %stack.224) | copy-start | bytes 196
  252.5 9.3 %copy-start.20 = (s16[2,16,1]{1,0,2:T(2,128)(2,1)S(1)}, s16[2,16,1]{1,0,2:T(2,128)(2,1)}, u32[]{:S(2)}) copy-start(s16[2,16,1]{1,0,2:T(2,128)(2,1)} %stack.223) | copy-start | bytes 196
  254.3 25.9 %all-to-all-start.3 = ((s16[32,72,256]{2,1,0:T(8,128)(2,1)}), s16[32,72,256]{2,1,0:T(8,128)(2,1)S(1)}, u32[]{:S(2)}, u32[]{:S(2)}) async-start(s16[32,72,256]{2,1,0:T(8,128)(2,1)} %bitcast.72), calls=%async_computation.3 | async-start | bytes 2359296 | tf_op jit(solution)/shard_map/all_to_all | solution.py:124
  263.5 2.3 copy-start.14
  263.6 2.3 copy-start.15
  263.6 2.3 copy-start.16
  263.6 2.3 copy-start.17
  282.2 1.9 copy-start
  284.1 1.9 copy-start.1
  286.0 1.9 copy-start.2
  287.9 1.9 copy-start.5
  289.8 1.9 copy-start.3
  291.7 2.9 copy-start.6
  294.5 1.9 copy-start.4
